TPU v7x, 32 devices: a whole 2x2x4 slice. The times are simulated.
32 devices in a mesh: section: 2 (over core), dp: 16 (over z, y, x).
Axes of the slice: x: 2, y: 2, z: 4, core: 2. Of those that a mesh axis runs over, the one named last changes fastest.
Arguments:
- images: bfloat16 [4, 16, 196, 512], P(None, 'dp'), may hold values from -6 to 6
- counts: int32 [4, 16], P(None, 'dp'), may hold values from 1 to 1, as said below
- shift_mask: int32 [4, 49, 49], replicated, may hold values from 0 to 1, as said below
- cotangent: bfloat16 [4, 16, 196, 512], P(None, 'dp'), may hold values from -6 to 6
- attention_gain: bfloat16 [2, 512], P('section', 'dp'), may hold values from 0.5 to 1.5
- attention_shift: bfloat16 [2, 512], P('section', 'dp'), may hold values from -3 to 3
- heads_weight: bfloat16 [2, 512, 1536], P('section', 'dp'), may hold values from -0.25 to 0.25
- query_bias: bfloat16 [2, 512], P('section', 'dp'), may hold values from -3 to 3
- value_bias: bfloat16 [2, 512], P('section', 'dp'), may hold values from -3 to 3
- merge_weight: bfloat16 [2, 512, 512], P('section', 'dp'), may hold values from -1 to 1
- merge_bias: bfloat16 [2, 512], P('section', 'dp'), may hold values from -3 to 3
- feed_gain: bfloat16 [2, 512], P('section', 'dp'), may hold values from 0.5 to 1.5
- feed_shift: bfloat16 [2, 512], P('section', 'dp'), may hold values from -3 to 3
- up_weight: bfloat16 [2, 512, 2048], P('section', 'dp'), may hold values from -0.25 to 0.25
- up_bias: bfloat16 [2, 2048], P('section', 'dp'), may hold values from -3 to 3
- down_weight: bfloat16 [2, 2048, 512], P('section', 'dp'), may hold values from -0.125 to 0.125
- down_bias: bfloat16 [2, 512], P('section', 'dp'), may hold values from -3 to 3
- bias_table: bfloat16 [2, 169, 16], P('section'), may hold values from -5 to 5
Outputs:
- layer_outputs: bfloat16 [2, 4, 16, 196, 512], P('section', None, 'dp')
- input_grads: float32 [2, 4, 16, 196, 512], P('section', None, 'dp')
- grad_attention_gain: float32 [2, 512], P('section', 'dp')
- grad_attention_shift: float32 [2, 512], P('section', 'dp')
- grad_heads_weight: float32 [2, 512, 1536], P('section', 'dp')
- grad_query_bias: float32 [2, 512], P('section', 'dp')
- grad_value_bias: float32 [2, 512], P('section', 'dp')
- grad_merge_weight: float32 [2, 512, 512], P('section', 'dp')
- grad_merge_bias: float32 [2, 512], P('section', 'dp')
- grad_feed_gain: float32 [2, 512], P('section', 'dp')
- grad_feed_shift: float32 [2, 512], P('section', 'dp')
- grad_up_weight: float32 [2, 512, 2048], P('section', 'dp')
- grad_up_bias: float32 [2, 2048], P('section', 'dp')
- grad_down_weight: float32 [2, 2048, 512], P('section', 'dp')
- grad_down_bias: float32 [2, 512], P('section', 'dp')
- grad_bias_table: float32 [2, 169, 16], P('section')
Inputs may be any that keep to these rules, and one draw needn't show every extreme that they name: Device d has 1 image slots in each micro-batch m, of which the first counts[m, d] hold images and the rest are empty; in every micro-batch some device fills all 1. `shift_mask`: for each window position, one row cut and one column cut split the window's tokens into rectangles; the mask is 1 between tokens of different rectangles and 0 within one (so symmetric, 0 on the diagonal).
All inputs are finite; a program needn't handle non-finite values.
Results may differ from a plain program's by a relative error of at most 0.017.
Values may be sent and summed in bfloat16 or wider, within the bound.
A program may use at most 192 MiB of HBM per device.

v0:
```python
import jax
import jax.numpy as jnp
from jax import lax
from jax.sharding import PartitionSpec as P

C = 512
HEADS = 16
HD = 32
WIN = 7
SIDE = 14
SHIFT = 3
WT = 49
NWIN = 4
TOKIMG = 196
TABLE = 169


EPSILON = 1e-05


def passed_along(value, axis, steps):
    count = lax.axis_size(axis)
    leading, last = (max(0, -steps), min(count, count - steps))
    return lax.ppermute(value, axis, [(source, source + steps) for source in range(leading, last)])


def layer_norm(values, norm_gain, offset):
    center = values - jnp.mean(values, -1, keepdims=True)
    spread = jnp.mean(center * center, -1, keepdims=True)
    return center * lax.rsqrt(spread + EPSILON) * norm_gain + offset


def gelu_exact(inputs):
    return jax.nn.gelu(inputs, approximate=False)


def relative_index():
    position = jnp.arange(WT, dtype=jnp.int32)
    rows_of = position // WIN
    cols_of = position % WIN
    return (
        (rows_of[:, None] - rows_of[None, :] + WIN - 1) * (2 * WIN - 1)
        + cols_of[:, None]
        - cols_of[None, :]
        + WIN
        - 1
    )


def to_windows(tokens, is_second):
    batch_size = tokens.shape[0]
    channels = tokens.shape[-1]
    square = tokens.reshape(batch_size, SIDE, SIDE, channels)
    square = jnp.where(is_second, jnp.roll(square, (-SHIFT, -SHIFT), (1, 2)), square)
    square = square.reshape(batch_size, SIDE // WIN, WIN, SIDE // WIN, WIN, channels)
    return square.transpose(0, 1, 3, 2, 4, 5).reshape(batch_size * NWIN, WT, channels)


def from_windows(windows, is_second):
    batch_size = windows.shape[0] // NWIN
    channels = windows.shape[-1]
    square = windows.reshape(batch_size, SIDE // WIN, SIDE // WIN, WIN, WIN, channels)
    square = square.transpose(0, 1, 3, 2, 4, 5).reshape(batch_size, SIDE, SIDE, channels)
    square = jnp.where(is_second, jnp.roll(square, (SHIFT, SHIFT), (1, 2)), square)
    return square.reshape(batch_size, TOKIMG, channels)


def widen(gathered):
    return tuple(
        (member.astype(jnp.float32) if member.ndim == 1 else member for member in gathered)
    )


def forward_pass(inputs, weights, pos_bias, mask_add, is_second):
    (
        attention_gain,
        attention_shift,
        heads_weight,
        query_bias,
        value_bias,
        merge_weight,
        merge_bias,
        feed_gain,
        feed_shift,
        up_weight,
        up_bias,
        down_weight,
        down_bias,
    ) = weights
    batch_size = inputs.shape[0]
    normed = layer_norm(inputs, attention_gain, attention_shift).astype(jnp.bfloat16)
    windowed = to_windows(normed, is_second)
    window_count = windowed.shape[0]
    project_bias = jnp.concatenate([query_bias, jnp.zeros_like(query_bias), value_bias])
    projected = (
        jnp.dot(windowed.reshape(-1, C), heads_weight, preferred_element_type=jnp.float32)
        + project_bias
    )
    projected = projected.astype(jnp.bfloat16).reshape(window_count, WT, 3, HEADS, HD)
    queries = projected[:, :, 0]
    key_vectors = projected[:, :, 1]
    value_vectors = projected[:, :, 2]
    scores = jnp.einsum(
        "wihd,wjhd->whij", queries, key_vectors, preferred_element_type=jnp.float32
    ) * HD ** (-0.5)
    scores = (
        scores.reshape(batch_size, NWIN, HEADS, WT, WT)
        + pos_bias[None, None]
        + mask_add[None, :, None]
    )
    attention = jax.nn.softmax(scores.reshape(window_count, HEADS, WT, WT), -1)
    mixed = jnp.einsum(
        "whij,wjhd->wihd",
        attention.astype(jnp.bfloat16),
        value_vectors,
        preferred_element_type=jnp.float32,
    )
    mixed = mixed.reshape(-1, C).astype(jnp.bfloat16)
    branch = jnp.dot(mixed, merge_weight, preferred_element_type=jnp.float32) + merge_bias
    middle = inputs + from_windows(branch.reshape(window_count, WT, C), is_second)
    normed_two = layer_norm(middle, feed_gain, feed_shift).astype(jnp.bfloat16).reshape(-1, C)
    hidden = jnp.dot(normed_two, up_weight, preferred_element_type=jnp.float32) + up_bias
    activated = gelu_exact(hidden).astype(jnp.bfloat16)
    result = middle + (
        jnp.dot(activated, down_weight, preferred_element_type=jnp.float32) + down_bias
    ).reshape(batch_size, TOKIMG, C)
    stored = (
        inputs,
        windowed,
        queries,
        key_vectors,
        value_vectors,
        attention,
        mixed,
        middle,
        normed_two,
        hidden,
        activated,
    )
    return (result, stored)


def backward_pass(upstream, weights, stored, one_hot, is_second):
    (
        attention_gain,
        attention_shift,
        heads_weight,
        query_bias,
        value_bias,
        merge_weight,
        merge_bias,
        feed_gain,
        feed_shift,
        up_weight,
        up_bias,
        down_weight,
        down_bias,
    ) = weights
    (
        inputs,
        windowed,
        queries,
        key_vectors,
        value_vectors,
        attention,
        mixed,
        middle,
        normed_two,
        hidden,
        activated,
    ) = stored
    batch_size = inputs.shape[0]
    window_count = windowed.shape[0]
    head_scale = HD ** (-0.5)
    grad_output = upstream.reshape(-1, C).astype(jnp.bfloat16)
    grad_down_bias = jnp.sum(grad_output, 0, dtype=jnp.float32)
    grad_down_weight = jnp.dot(activated.T, grad_output, preferred_element_type=jnp.float32)
    grad_activated = jnp.dot(grad_output, down_weight.T, preferred_element_type=jnp.float32)
    gelu_back = jax.vjp(gelu_exact, hidden)[1]
    grad_hidden = gelu_back(grad_activated)[0].astype(jnp.bfloat16)
    grad_up_bias = jnp.sum(grad_hidden, 0, dtype=jnp.float32)
    grad_up_weight = jnp.dot(normed_two.T, grad_hidden, preferred_element_type=jnp.float32)
    grad_normed_two = jnp.dot(grad_hidden, up_weight.T, preferred_element_type=jnp.float32)
    feed_back = jax.vjp(layer_norm, middle, feed_gain, feed_shift)[1]
    grad_middle, grad_feed_gain, grad_feed_shift = feed_back(
        grad_normed_two.reshape(batch_size, TOKIMG, C)
    )
    grad_middle = grad_middle + upstream
    grad_branch = to_windows(grad_middle.astype(jnp.bfloat16), is_second).reshape(-1, C)
    grad_merge_bias = jnp.sum(grad_branch, 0, dtype=jnp.float32)
    grad_merge_weight = jnp.dot(mixed.T, grad_branch, preferred_element_type=jnp.float32)
    grad_mixed = jnp.dot(grad_branch, merge_weight.T, preferred_element_type=jnp.float32)
    grad_mixed = grad_mixed.astype(jnp.bfloat16).reshape(window_count, WT, HEADS, HD)
    grad_attention = jnp.einsum(
        "wihd,wjhd->whij", grad_mixed, value_vectors, preferred_element_type=jnp.float32
    )
    grad_values = jnp.einsum(
        "whij,wihd->wjhd",
        attention.astype(jnp.bfloat16),
        grad_mixed,
        preferred_element_type=jnp.float32,
    ).astype(jnp.bfloat16)
    row_total = jnp.sum(grad_attention * attention, -1, keepdims=True)
    grad_scores = (attention * (grad_attention - row_total)).astype(jnp.bfloat16)
    grad_bias = jnp.sum(grad_scores, 0, dtype=jnp.float32)
    grad_table = jnp.dot(
        one_hot.T,
        grad_bias.transpose(1, 2, 0).reshape(WT * WT, HEADS),
        precision=lax.Precision.HIGHEST,
    )
    grad_queries = (
        jnp.einsum("whij,wjhd->wihd", grad_scores, key_vectors, preferred_element_type=jnp.float32)
        * head_scale
    ).astype(jnp.bfloat16)
    grad_keys = (
        jnp.einsum("whij,wihd->wjhd", grad_scores, queries, preferred_element_type=jnp.float32)
        * head_scale
    ).astype(jnp.bfloat16)
    grad_projected = jnp.stack([grad_queries, grad_keys, grad_values], 2).reshape(-1, 3 * C)
    grad_query_bias = jnp.sum(grad_queries, (0, 1), dtype=jnp.float32).reshape(C)
    grad_value_bias = jnp.sum(grad_values, (0, 1), dtype=jnp.float32).reshape(C)
    grad_heads_weight = jnp.dot(
        windowed.reshape(-1, C).T, grad_projected, preferred_element_type=jnp.float32
    )
    grad_normed = jnp.dot(grad_projected, heads_weight.T, preferred_element_type=jnp.float32)
    grad_normed = from_windows(grad_normed.reshape(window_count, WT, C), is_second)
    attention_back = jax.vjp(layer_norm, inputs, attention_gain, attention_shift)[1]
    grad_inputs, grad_attention_gain, grad_attention_shift = attention_back(grad_normed)
    grad_inputs = grad_inputs + grad_middle
    local_grads = (
        grad_attention_gain,
        grad_attention_shift,
        grad_heads_weight,
        grad_query_bias,
        grad_value_bias,
        grad_merge_weight,
        grad_merge_bias,
        grad_feed_gain,
        grad_feed_shift,
        grad_up_weight,
        grad_up_bias,
        grad_down_weight,
        grad_down_bias,
    )
    return (local_grads, grad_table, grad_inputs)


def add_pair(former, latter):
    return former + latter


def shards(
    images,
    counts,
    shift_mask,
    cotangent,
    attention_gain,
    attention_shift,
    heads_weight,
    query_bias,
    value_bias,
    merge_weight,
    merge_bias,
    feed_gain,
    feed_shift,
    up_weight,
    up_bias,
    down_weight,
    down_bias,
    bias_table,
):
    section_index = lax.axis_index("section")
    is_second = section_index == 1
    section_flag = is_second.astype(jnp.float32)
    micro_count = images.shape[0]
    slot_count = images.shape[1]
    index_table = relative_index().reshape(-1)
    one_hot = (index_table[:, None] == jnp.arange(TABLE, dtype=jnp.int32)[None, :]).astype(
        jnp.float32
    )
    table_values = bias_table[0].astype(jnp.float32)
    pos_bias = jnp.dot(one_hot, table_values, precision=lax.Precision.HIGHEST)
    pos_bias = pos_bias.reshape(WT, WT, HEADS).transpose(2, 0, 1)
    mask_add = -100.0 * section_flag * shift_mask.astype(jnp.float32)
    live_rows = (jnp.arange(slot_count, dtype=jnp.int32)[None, :] < counts).astype(jnp.float32)
    no_rows = jnp.zeros((slot_count,), jnp.float32)
    forward_weights = widen(
        (
            lax.all_gather(attention_gain[0], "dp", axis=0, tiled=True),
            lax.all_gather(attention_shift[0], "dp", axis=0, tiled=True),
            lax.all_gather(heads_weight[0], "dp", axis=0, tiled=True),
            lax.all_gather(query_bias[0], "dp", axis=0, tiled=True),
            lax.all_gather(value_bias[0], "dp", axis=0, tiled=True),
            lax.all_gather(merge_weight[0], "dp", axis=0, tiled=True),
            lax.all_gather(merge_bias[0], "dp", axis=0, tiled=True),
            lax.all_gather(feed_gain[0], "dp", axis=0, tiled=True),
            lax.all_gather(feed_shift[0], "dp", axis=0, tiled=True),
            lax.all_gather(up_weight[0], "dp", axis=0, tiled=True),
            lax.all_gather(up_bias[0], "dp", axis=0, tiled=True),
            lax.all_gather(down_weight[0], "dp", axis=0, tiled=True),
            lax.all_gather(down_bias[0], "dp", axis=0, tiled=True),
        )
    )
    received = jnp.zeros((slot_count, TOKIMG, C), jnp.bfloat16)
    kept_list = []
    output_list = []
    for tick_index in range(micro_count + 1):
        if tick_index < micro_count:
            own_input = images[tick_index]
            live_first = live_rows[tick_index]
        else:
            own_input = jnp.zeros((slot_count, TOKIMG, C), jnp.bfloat16)
            live_first = no_rows
        live_second = live_rows[tick_index - 1] if tick_index > 0 else no_rows
        live_now = jnp.where(is_second, live_second, live_first)
        source = jnp.where(is_second, received, own_input).astype(jnp.float32)
        result, stored = forward_pass(source, forward_weights, pos_bias, mask_add, is_second)
        result = (result * live_now[:, None, None]).astype(jnp.bfloat16)
        kept_list.append((stored, live_now))
        output_list.append(result)
        if tick_index < micro_count:
            received = passed_along(result, "section", 1)
    stacked_out = jnp.stack(output_list)
    layer_outputs = jnp.where(is_second, stacked_out[1:], stacked_out[:micro_count])[None]
    backward_weights = widen(
        (
            lax.all_gather(attention_gain[0], "dp", axis=0, tiled=True),
            lax.all_gather(attention_shift[0], "dp", axis=0, tiled=True),
            lax.all_gather(heads_weight[0], "dp", axis=0, tiled=True),
            lax.all_gather(query_bias[0], "dp", axis=0, tiled=True),
            lax.all_gather(value_bias[0], "dp", axis=0, tiled=True),
            lax.all_gather(merge_weight[0], "dp", axis=0, tiled=True),
            lax.all_gather(merge_bias[0], "dp", axis=0, tiled=True),
            lax.all_gather(feed_gain[0], "dp", axis=0, tiled=True),
            lax.all_gather(feed_shift[0], "dp", axis=0, tiled=True),
            lax.all_gather(up_weight[0], "dp", axis=0, tiled=True),
            lax.all_gather(up_bias[0], "dp", axis=0, tiled=True),
            lax.all_gather(down_weight[0], "dp", axis=0, tiled=True),
            lax.all_gather(down_bias[0], "dp", axis=0, tiled=True),
        )
    )
    received_grad = jnp.zeros((slot_count, TOKIMG, C), jnp.bfloat16)
    table_local = jnp.zeros((TABLE, HEADS), jnp.float32)
    grad_list = []
    shares_total = None
    for turn_index in range(micro_count + 1):
        stored, live_now = kept_list[micro_count - turn_index]
        if turn_index < micro_count:
            own_grad = cotangent[micro_count - 1 - turn_index].astype(jnp.float32)
        else:
            own_grad = jnp.zeros((slot_count, TOKIMG, C), jnp.float32)
        upstream = (
            jnp.where(is_second, own_grad, received_grad.astype(jnp.float32))
            * live_now[:, None, None]
        )
        local_grads, grad_table, grad_inputs = backward_pass(
            upstream, backward_weights, stored, one_hot, is_second
        )
        table_local = table_local + grad_table
        sent_grad = grad_inputs.astype(jnp.bfloat16)
        grad_list.append(jnp.where(is_second, sent_grad.astype(jnp.float32), grad_inputs))
        if turn_index < micro_count:
            received_grad = passed_along(sent_grad, "section", -1)
        shares = (
            lax.psum_scatter(local_grads[0], "dp", scatter_dimension=0, tiled=True),
            lax.psum_scatter(local_grads[1], "dp", scatter_dimension=0, tiled=True),
            lax.psum_scatter(local_grads[2], "dp", scatter_dimension=0, tiled=True),
            lax.psum_scatter(local_grads[3], "dp", scatter_dimension=0, tiled=True),
            lax.psum_scatter(local_grads[4], "dp", scatter_dimension=0, tiled=True),
            lax.psum_scatter(local_grads[5], "dp", scatter_dimension=0, tiled=True),
            lax.psum_scatter(local_grads[6], "dp", scatter_dimension=0, tiled=True),
            lax.psum_scatter(local_grads[7], "dp", scatter_dimension=0, tiled=True),
            lax.psum_scatter(local_grads[8], "dp", scatter_dimension=0, tiled=True),
            lax.psum_scatter(local_grads[9], "dp", scatter_dimension=0, tiled=True),
            lax.psum_scatter(local_grads[10], "dp", scatter_dimension=0, tiled=True),
            lax.psum_scatter(local_grads[11], "dp", scatter_dimension=0, tiled=True),
            lax.psum_scatter(local_grads[12], "dp", scatter_dimension=0, tiled=True),
        )
        shares_total = (
            shares if shares_total is None else jax.tree.map(add_pair, shares_total, shares)
        )
    table_grad = lax.psum(table_local, "dp")[None]
    reversed_grads = jnp.stack(grad_list[::-1])
    input_grads = jnp.where(is_second, reversed_grads[1:], reversed_grads[:micro_count])[None]
    return (
        layer_outputs,
        input_grads,
        shares_total[0][None],
        shares_total[1][None],
        shares_total[2][None],
        shares_total[3][None],
        shares_total[4][None],
        shares_total[5][None],
        shares_total[6][None],
        shares_total[7][None],
        shares_total[8][None],
        shares_total[9][None],
        shares_total[10][None],
        shares_total[11][None],
        shares_total[12][None],
        table_grad,
    )


def solution(mesh):
    return jax.shard_map(
        shards,
        mesh=mesh,
        in_specs=(
            P(None, "dp", None, None),
            P(None, "dp"),
            P(),
            P(None, "dp", None, None),
            P("section", "dp"),
            P("section", "dp"),
            P("section", "dp", None),
            P("section", "dp"),
            P("section", "dp"),
            P("section", "dp", None),
            P("section", "dp"),
            P("section", "dp"),
            P("section", "dp"),
            P("section", "dp", None),
            P("section", "dp"),
            P("section", "dp", None),
            P("section", "dp"),
            P("section", None, None),
        ),
        out_specs=(
            P("section", None, "dp", None, None),
            P("section", None, "dp", None, None),
            P("section", "dp"),
            P("section", "dp"),
            P("section", "dp", None),
            P("section", "dp"),
            P("section", "dp"),
            P("section", "dp", None),
            P("section", "dp"),
            P("section", "dp"),
            P("section", "dp"),
            P("section", "dp", None),
            P("section", "dp"),
            P("section", "dp", None),
            P("section", "dp"),
            P("section", None, None),
        ),
        check_vma=False,
    )
```

profile of v0, /device:TPU:0, one launch (start us, length us, event | category | flops | bytes accessed | tf_op | source)
XLA Modules:
  0.0 1070.3 jit_solution(14486843201174761786)
XLA Ops:
  9.5 4.7 fusion.539
  19.1 44.1 %all-reduce.18 = (bf16[512]{0:T(512)(128)(2,1)S(1)}, bf16[512]{0:T(512)(128)(2,1)S(1)}, bf16[512]{0:T(512)(128)(2,1)S(1)}, bf16[512]{0:T(512)(128)(2,1)S(1)}, bf...) all-reduce(bf16[512]{0:T(512)(128)(2,1)S(1)} %dynamic-update-slice., ...), channel_id=3, replica_groups=mesh['section'=2,'dp'=16] {'dp'}, use_global_device_ids=true, to_apply=%add.1 | all-reduce | flops 4096 | bytes 16384
  69.3 39.4 %all-gather.5 = bf16[1,512,512]{2,1,0:T(8,128)(2,1)S(1)} all-gather(bf16[1,32,512]{2,1,0:T(8,128)(2,1)S(1)} %copy-done.194), channel_id=7, replica_groups=mesh['section'=2,'dp'=16] {'dp'}, dimensions={1}, use_global_device_ids=true | all-gather | bytes 557056 | tf_op jit(solution)/shard_map/all_gather | solution.py:294
  108.8 37.2 %all-gather.10 = bf16[1,2048]{1,0:T(2,128)(2,1)S(1)} all-gather(bf16[1,128]{1,0:T(2,128)(2,1)S(1)} %copy-done.296), channel_id=12, replica_groups=mesh['section'=2,'dp'=16] {'dp'}, dimensions={1}, use_global_device_ids=true | all-gather | bytes 4352 | tf_op jit(solution)/shard_map/all_gather | solution.py:299
  168.9 7.3 multiply_convert_fusion.9
  176.1 21.3 %all-gather.21.cloned.1.call-done = bf16[1,2048,512]{2,1,0:T(8,128)(2,1)} async-done(((bf16[1,128,512]{2,1,0:T(8,128)(2,1)}), bf16[1,2048,512]{2,1,0:T(8,128)(2,1)}) %all-gather.21.cloned.1.call-update) | async-done | bytes 2097168 | tf_op jit(solution)/shard_map/all_gather | solution.py:300
  228.7 5.6 multiply_convert_fusion.8
  268.4 5.6 multiply_convert_fusion.7
  318.8 5.6 multiply_convert_fusion.6
  378.7 4.9 multiply_convert_fusion.5
  416.6 4.7 copy.448
  478.5 4.7 copy.449
  500.6 4.6 convolution_add_fusion.3
  541.5 4.7 copy.450
  546.1 4.6 reshape.3163
  563.9 4.5 convolution_add_fusion.2
  601.2 4.8 copy.451
  606.0 4.7 reshape.3164
  623.1 4.6 convolution_add_fusion.1
  723.6 5.0 copy.452
  743.0 75.1 %all-reduce.17 = (f32[512]{0:T(512)S(1)}, f32[512]{0:T(512)S(1)}, f32[512]{0:T(512)S(1)}, f32[512]{0:T(512)S(1)}, f32[512]{0:T(512)S(1)}, /*index=5*/f32[512]{0:...) all-reduce(f32[512]{0:T(512)S(1)} %add_add_fusion.33, ...), channel_id=67, replica_groups=mesh['section'=2,'dp'=16] {'dp'}, use_global_device_ids=true, to_apply=%region_56.57.clone | all-reduce | flops 8848 | bytes 70784
  823.4 45.0 %reduce-scatter.5.cloned.1.call-done = f32[32,1536]{1,0:T(8,128)} async-done(((f32[512,1536]{1,0:T(8,128)}), f32[32,1536]{1,0:T(8,128)}) %reduce-scatter.5.cloned.1.call-update) | async-done | bytes 196624 | tf_op jit(solution)/shard_map/reduce_scatter | solution.py:367
  868.3 97.2 %reduce-scatter.9.cloned.1.call-done = f32[32,2048]{1,0:T(8,128)} async-done(((f32[512,2048]{1,0:T(8,128)}), f32[32,2048]{1,0:T(8,128)}) %reduce-scatter.9.cloned.1.call-update) | async-done | bytes 262160 | tf_op jit(solution)/shard_map/reduce_scatter | solution.py:374
  965.6 97.7 %reduce-scatter.11.cloned.1.call-done = f32[128,512]{1,0:T(8,128)} async-done(((f32[2048,512]{1,0:T(8,128)}), f32[128,512]{1,0:T(8,128)}) %reduce-scatter.11.cloned.1.call-update) | async-done | bytes 262160 | tf_op jit(solution)/shard_map/reduce_scatter | solution.py:376
  (1159 shorter events, 506.7 us)
Async XLA Ops:
  7.2 60.3 %copy-start = (bf16[1,169,16]{1,2,0:T(8,128)(2,1)S(1)}, bf16[1,169,16]{1,2,0:T(8,128)(2,1)}, u32[]{:S(2)}) copy-start(bf16[1,169,16]{1,2,0:T(8,128)(2,1)} %param.35) | copy-start | bytes 16228
  7.2 140.2 %all-gather.17.cloned.1.call-start = ((), (), s32[]{:S(2)}) async-start(), calls=%async_computation.4 | async-start | bytes 1671168 | tf_op jit(solution)/shard_map/all_gather | solution.py:291
  7.9 160.9 %all-gather.19.cloned.1.call-start = ((), (), s32[]{:S(2)}) async-start(), calls=%async_computation.5 | async-start | bytes 2228224 | tf_op jit(solution)/shard_map/all_gather | solution.py:298
  8.7 188.8 %all-gather.21.cloned.1.call-start = ((), (), s32[]{:S(2)}) async-start(), calls=%async_computation.6 | async-start | bytes 2228224 | tf_op jit(solution)/shard_map/all_gather | solution.py:300
  9.4 813.9 %reduce-scatter.7.cloned.1.call-start = ((), (), s32[]{:S(2)}) async-start(), calls=%async_computation.8 | async-start | bytes 1114112 | tf_op jit(solution)/shard_map/reduce_scatter | solution.py:370
  14.4 154.3 %copy-start.11 = (bf16[1,1,196,512]{3,2,1,0:T(8,128)(2,1)}, bf16[1,1,196,512]{3,2,1,0:T(8,128)(2,1)S(1)}, u32[]{:S(2)}) copy-start(bf16[1,1,196,512]{3,2,1,0:T(8,128)(2,1)S(1)} %get-tuple-element.184) | copy-start | bytes 602116
  15.5 50.6 %copy-start.169 = (f32[196]{0:T(256)}, f32[196]{0:T(256)S(1)}, u32[]{:S(2)}) copy-start(f32[196]{0:T(256)S(1)} %broadcast_multiply_fusion.9) | copy-start | bytes 2356
  66.4 79.6 %copy-start.313 = (s32[4,1]{0,1:T(1,128)S(1)}, s32[4,1]{0,1:T(1,128)}, u32[]{:S(2)}) copy-start(s32[4,1]{0,1:T(1,128)} %param.19) | copy-start | bytes 52
  66.5 82.8 %copy-start.102 = (bf16[196,512]{1,0:T(8,128)(2,1)}, bf16[196,512]{1,0:T(8,128)(2,1)S(1)}, u32[]{:S(2)}) copy-start(bf16[196,512]{1,0:T(8,128)(2,1)S(1)} %reshape_reshape.55) | copy-start | bytes 602116
  67.5 81.8 %copy-start.159 = (s32[49,49]{1,0:T(8,128)}, s32[49,49]{1,0:T(8,128)S(1)}, u32[]{:S(2)}) copy-start(s32[49,49]{1,0:T(8,128)S(1)} %subtract_add_fusion) | copy-start | bytes 28816
  108.8 115.8 %copy-start.165 = (f32[512]{0:T(512)}, f32[512]{0:T(512)S(1)}, u32[]{:S(2)}) copy-start(f32[512]{0:T(512)S(1)} %convert_element_type.877) | copy-start | bytes 6148
  146.1 51.4 %copy-start.289 = (f32[512]{0:T(512)}, f32[512]{0:T(512)S(1)}, u32[]{:S(2)}) copy-start(f32[512]{0:T(512)S(1)} %convert_element_type.880) | copy-start | bytes 6148
  199.7 2.8 collective-permute-start
  235.3 3.6 collective-permute-start.1
  274.9 3.0 collective-permute-start.2
  325.3 6.0 collective-permute-start.3
  433.4 10.0 collective-permute-start.4
  495.3 11.2 %collective-permute-start.5 = (bf16[1,196,512]{2,1,0:T(8,128)(2,1)}, bf16[1,196,512]{2,1,0:T(8,128)(2,1)}, u32[]{:S(2)}, u32[]{:S(2)}) collective-permute-start(bf16[1,196,512]{2,1,0:T(8,128)(2,1)} %get-tuple-element.206), channel_id=1, source_target_pairs={{16,0},{17,1},{18,2},{19,3},{20,4},{21,5},{22,6},{23,7},{24,8},{25... | collective-permute-start | bytes 602120 | tf_op jit(solution)/shard_map/ppermute | solution.py:24
  559.1 10.7 collective-permute-start.6
  618.3 10.7 %collective-permute-start.7 = (bf16[1,196,512]{2,1,0:T(8,128)(2,1)}, bf16[1,196,512]{2,1,0:T(8,128)(2,1)S(1)}, u32[]{:S(2)}, u32[]{:S(2)}) collective-permute-start(bf16[1,196,512]{2,1,0:T(8,128)(2,1)} %get-tuple-element.202), channel_id=1, source_target_pairs={{16,0},{17,1},{18,2},{19,3},{20,4},{21,5},{22,6},{23,7},{24,8},{25... | collective-permute-start | bytes 602120 | tf_op jit(solution)/shard_map/ppermute | solution.py:24
  656.0 212.4 %reduce-scatter.5.cloned.1.call-start = ((), (), s32[]{:S(2)}) async-start(), calls=%async_computation.7 | async-start | bytes 3342336 | tf_op jit(solution)/shard_map/reduce_scatter | solution.py:367
  675.8 289.7 %reduce-scatter.9.cloned.1.call-start = ((), (), s32[]{:S(2)}) async-start(), calls=%async_computation.9 | async-start | bytes 4456448 | tf_op jit(solution)/shard_map/reduce_scatter | solution.py:374
  685.9 377.3 %reduce-scatter.11.cloned.1.call-start = ((), (), s32[]{:S(2)}) async-start(), calls=%async_computation.10 | async-start | bytes 4456448 | tf_op jit(solution)/shard_map/reduce_scatter | solution.py:376
  739.8 323.4 %copy-start.1 = (bf16[1,169,16]{1,2,0:T(8,128)(2,1)S(1)}, bf16[1,169,16]{1,2,0:T(8,128)(2,1)}, u32[]{:S(2)}) copy-start(bf16[1,169,16]{1,2,0:T(8,128)(2,1)} %param.35) | copy-start | bytes 16228
  (316 other events, 1050.0 us)
Sparse Core Ops, SparseCore 0:
  10.8 61.4 all-gather.16
  75.1 60.2 all-gather.18
  138.2 59.2 all-gather.20
  656.1 78.9 reduce-scatter.6
  741.3 127.0 reduce-scatter.4
  871.2 94.3 reduce-scatter.8
  968.5 94.7 reduce-scatter.10
where the time goes:
time: 1080 us; the launch traced here: 1070 us
  local copies, waits for them, and re-layouts  304 us (28%)
  waiting for transfers between devices  263 us (24%)
  blocking collectives  196 us (18%)
  matrix products  188 us (17%)
  other arithmetic  79.7 us (7%)
  between operations  26 us (2%)
  starting transfers between devices  13.3 us (1%)
    unnamed x2, blocking collectives  119 us
    reduce_scatter x1, waiting for transfers between devices, shards(): lax.psum_scatter(local_grads[11], 'dp', scatter_dimension=0, tiled=True)  97.7 us
    reduce_scatter x1, waiting for transfers between devices, shards(): lax.psum_scatter(local_grads[9], 'dp', scatter_dimension=0, tiled=True)  97.2 us
    unnamed x684, local copies, waits for them, and re-layouts  63.8 us
    another operation x11, local copies, waits for them, and re-layouts  45.8 us
    reduce_scatter x1, waiting for transfers between devices, shards(): lax.psum_scatter(local_grads[2], 'dp', scatter_dimension=0, tiled=True)  45 us
    all_gather x1, blocking collectives, shards(): lax.all_gather(merge_weight[0], 'dp', axis=0, tiled=True)  39.4 us
    all_gather x1, blocking collectives, shards(): lax.all_gather(up_bias[0], 'dp', axis=0, tiled=True)  37.2 us
  transfers between devices with their start and end apart: 15, of which 4 were waited for; matrix products, arithmetic and copies ran while one was open for 15% of the time, Pallas kernels for 0%

commit v1 on v0

v1 whole, which is shorter than its diff:
```python
import jax
import jax.numpy as jnp
from jax import lax
from jax.experimental import pallas as pl
from jax.experimental.pallas import tpu as pltpu
from jax.sharding import PartitionSpec as P

C = 512
HEADS = 16
HD = 32
FF = 2048
WIN = 7
SIDE = 14
SHIFT = 3
WT = 49
NWIN = 4
TOKIMG = 196
TABLE = 169
EPSILON = 1e-05

PW = 64
ROWS = NWIN * PW
GROUPS = 4
TILES = 12
SCALE = HD ** (-0.5)
F32 = jnp.float32
BF16 = jnp.bfloat16
VMEM_BYTES = 56 * 1024 * 1024


def dot(a, b):
    return jnp.dot(a, b, preferred_element_type=F32)


def dot_nt(a, b):
    return lax.dot_general(a, b, (((1,), (1,)), ((), ())), preferred_element_type=F32)


def dot_tn(a, b):
    return lax.dot_general(a, b, (((0,), (0,)), ((), ())), preferred_element_type=F32)


def normalise(values):
    center = values - jnp.mean(values, -1, keepdims=True)
    rstd = lax.rsqrt(jnp.mean(center * center, -1, keepdims=True) + EPSILON)
    return center * rstd, rstd


def weight_tile(w_ref, c):
    return w_ref[:, c].reshape(C, C)


def down_tile(w_ref, c):
    n = w_ref.shape[0] // 4
    return w_ref[c * n : (c + 1) * n, 8:12].reshape(C, C)


def head_of_lane():
    return lax.broadcasted_iota(jnp.int32, (PW, 128), 1) // HD


def spread_heads(block, lane_head):
    zero = jnp.zeros_like(block)
    return jnp.concatenate([jnp.where(lane_head == h, block, zero) for h in range(4)], 0)


def pick_heads(stack, lane_head):
    out = stack[0:PW]
    for h in range(1, 4):
        out = jnp.where(lane_head == h, stack[h * PW : (h + 1) * PW], out)
    return out


def forward_body(
    x_ref, live_ref, perm_ref, permt_ref, bias_ref, w_ref, vec_ref, pb_ref, ub_ref,
    out_ref, xw_ref, h_ref, qkv_ref, a_ref, r_ref, x1_ref, h2_ref, z_ref, gp_ref,
):
    x = dot(perm_ref[...], x_ref[...])
    xw_ref[...] = x.astype(BF16)
    n1, _ = normalise(x)
    h = (n1 * vec_ref[0:1] + vec_ref[1:2]).astype(BF16)
    h_ref[...] = h
    for c in range(3):
        cols = slice(c * C, (c + 1) * C)
        qkv_ref[:, cols] = (dot(h, weight_tile(w_ref, c)) + pb_ref[:, cols]).astype(BF16)
    lane_head = head_of_lane()
    for w in range(NWIN):
        rows = slice(w * PW, (w + 1) * PW)
        for g in range(GROUPS):
            lanes = g * 128
            q = qkv_ref[rows, lanes : lanes + 128]
            k = qkv_ref[rows, C + lanes : C + lanes + 128]
            v = qkv_ref[rows, 2 * C + lanes : 2 * C + lanes + 128]
            st = dot_nt(k, spread_heads(q, lane_head)) * SCALE + bias_ref[w * GROUPS + g]
            e = jnp.exp(st - jnp.max(st, 0, keepdims=True))
            a = (e * (1.0 / jnp.sum(e, 0, keepdims=True))).astype(BF16)
            a_ref[w * GROUPS + g] = a
            r_ref[rows, lanes : lanes + 128] = pick_heads(dot_tn(a, v), lane_head).astype(BF16)
    x1 = x + (dot(r_ref[...], weight_tile(w_ref, 3)) + vec_ref[2:3])
    x1_ref[...] = x1
    n2, _ = normalise(x1)
    h2 = (n2 * vec_ref[3:4] + vec_ref[4:5]).astype(BF16)
    h2_ref[...] = h2
    total = x1 + vec_ref[5:6]
    for c in range(4):
        cols = slice(c * C, (c + 1) * C)
        g = dot(h2, weight_tile(w_ref, 4 + c)) + ub_ref[:, cols]
        cdf = 0.5 + 0.5 * lax.erf(g * (0.5**0.5))
        pdf = jnp.exp(-0.5 * g * g) * 0.3989422804014327
        z = (g * cdf).astype(BF16)
        z_ref[:, cols] = z
        gp_ref[:, cols] = (cdf + g * pdf).astype(BF16)
        total = total + dot(z, down_tile(w_ref, c))
    out = (total * live_ref[0, 0]).astype(BF16)
    out_ref[...] = dot(permt_ref[...], out).astype(BF16)


def backward_body(
    e_ref, live_ref, perm_ref, permt_ref, w_ref, vec_ref,
    xw_ref, qkv_ref, a_ref, x1_ref, gp_ref,
    dx_ref, sent_ref, do_ref, dg_ref, db_ref, dp_ref, vg_ref, ug_ref, ds_ref,
    dr_ref,
):
    e = dot(perm_ref[...], e_ref[...]) * live_ref[0, 0]
    do = e.astype(BF16)
    do_ref[...] = do
    dh2 = jnp.zeros((ROWS, C), F32)
    for c in range(4):
        cols = slice(c * C, (c + 1) * C)
        dz = dot_nt(do, down_tile(w_ref, c))
        dg = (dz * gp_ref[:, cols].astype(F32)).astype(BF16)
        dg_ref[:, cols] = dg
        ug_ref[:, cols] = jnp.sum(dg.astype(F32), 0, keepdims=True)
        dh2 = dh2 + dot_nt(dg, weight_tile(w_ref, 4 + c))
    n2, r2 = normalise(x1_ref[...])
    d = dh2 * vec_ref[3:4]
    dx1 = e + r2 * (
        d - jnp.mean(d, -1, keepdims=True) - n2 * jnp.mean(d * n2, -1, keepdims=True)
    )
    db = dx1.astype(BF16)
    db_ref[...] = db
    dr_ref[...] = dot_nt(db, weight_tile(w_ref, 3)).astype(BF16)
    lane_head = head_of_lane()
    for w in range(NWIN):
        rows = slice(w * PW, (w + 1) * PW)
        for g in range(GROUPS):
            lanes = g * 128
            q = qkv_ref[rows, lanes : lanes + 128]
            k = qkv_ref[rows, C + lanes : C + lanes + 128]
            v = qkv_ref[rows, 2 * C + lanes : 2 * C + lanes + 128]
            a = a_ref[w * GROUPS + g]
            drs = spread_heads(dr_ref[rows, lanes : lanes + 128], lane_head)
            da = dot_nt(v, drs)
            dv = dot(a, drs)
            af = a.astype(F32)
            pa = da * af
            ds = (pa - af * jnp.sum(pa, 0, keepdims=True)).astype(BF16)
            if w == 0:
                ds_ref[g] = ds.astype(F32)
            else:
                ds_ref[g] += ds.astype(F32)
            dq = pick_heads(dot_tn(ds, k), lane_head) * SCALE
            dk = dot(ds, spread_heads(q, lane_head)) * SCALE
            dp_ref[rows, lanes : lanes + 128] = dq.astype(BF16)
            dp_ref[rows, C + lanes : C + lanes + 128] = dk.astype(BF16)
            dp_ref[rows, 2 * C + lanes : 2 * C + lanes + 128] = dv.astype(BF16)
    dh = jnp.zeros((ROWS, C), F32)
    for c in range(3):
        dh = dh + dot_nt(dp_ref[:, c * C : (c + 1) * C], weight_tile(w_ref, c))
    n1, r1 = normalise(xw_ref[...].astype(F32))
    d = dh * vec_ref[0:1]
    dx = dx1 + r1 * (
        d - jnp.mean(d, -1, keepdims=True) - n1 * jnp.mean(d * n1, -1, keepdims=True)
    )
    high = dx.astype(BF16)
    low = (dx - high.astype(F32)).astype(BF16)
    top = dot(permt_ref[...], high)
    dx_ref[...] = top + dot(permt_ref[...], low)
    sent_ref[...] = top.astype(BF16)

    def column_sum(value):
        return jnp.sum(value.astype(F32), 0, keepdims=True)

    vg_ref[0:1] = column_sum(dh * n1)
    vg_ref[1:2] = column_sum(dh)
    vg_ref[2:3] = column_sum(dp_ref[:, 0:C])
    vg_ref[3:4] = column_sum(dp_ref[:, 2 * C :])
    vg_ref[4:5] = column_sum(db)
    vg_ref[5:6] = column_sum(dh2 * n2)
    vg_ref[6:7] = column_sum(dh2)
    vg_ref[7:8] = column_sum(do)


def weight_grads_body(count, *refs):
    h, r, h2, z, do, dg, db, dp = (refs[i * count : (i + 1) * count] for i in range(8))
    out_ref = refs[8 * count]
    owners = out_ref.shape[0]

    def product(left, lcols, right, rcols):
        total = dot_tn(left[0][:, lcols], right[0][:, rcols])
        for l, r_ in zip(left[1:], right[1:]):
            total = total + dot_tn(l[:, lcols], r_[:, rcols])
        return total.astype(BF16)

    whole = slice(0, C)
    for c in range(3):
        cols = slice(c * C, (c + 1) * C)
        out_ref[:, c] = product(h, whole, dp, cols).reshape(owners, C // owners, C)
    out_ref[:, 3] = product(r, whole, db, whole).reshape(owners, C // owners, C)
    for c in range(4):
        cols = slice(c * C, (c + 1) * C)
        out_ref[:, 4 + c] = product(h2, whole, dg, cols).reshape(owners, C // owners, C)
        n = owners // 4
        out_ref[c * n : (c + 1) * n, 8:12] = product(z, cols, do, whole).reshape(
            n, 4, C // owners, C
        )


def call(body, outs, args, scratch=(), smem=(), flops=0):
    vmem = pl.BlockSpec(memory_space=pltpu.VMEM)
    return pl.pallas_call(
        body,
        out_shape=[jax.ShapeDtypeStruct(s, d) for s, d in outs],
        in_specs=[
            pl.BlockSpec(memory_space=pltpu.SMEM) if i in smem else vmem for i in range(len(args))
        ],
        out_specs=[vmem] * len(outs),
        scratch_shapes=list(scratch),
        compiler_params=pltpu.CompilerParams(vmem_limit_bytes=VMEM_BYTES),
        cost_estimate=pl.CostEstimate(flops=flops, bytes_accessed=16 << 20, transcendentals=0),
    )(*args)


def relative_index():
    position = jnp.arange(WT, dtype=jnp.int32)
    rows_of, cols_of = position // WIN, position % WIN
    return (
        (rows_of[:, None] - rows_of[None, :] + WIN - 1) * (2 * WIN - 1)
        + cols_of[:, None]
        - cols_of[None, :]
        + WIN
        - 1
    )


def token_of_row(is_second):
    row = jnp.arange(ROWS, dtype=jnp.int32)
    window, place = row // PW, row % PW
    shift = jnp.where(is_second, SHIFT, 0)
    r = (window // 2 * WIN + place // WIN + shift) % SIDE
    c = (window % 2 * WIN + place % WIN + shift) % SIDE
    return jnp.where(place < WT, r * SIDE + c, -1)


def pad_pairs(values):
    lead = [(0, 0)] * (values.ndim - 2)
    return jnp.pad(jnp.swapaxes(values, -1, -2), lead + [(0, PW - WT), (0, PW - WT)])


def shards(
    images, counts, shift_mask, cotangent, attention_gain, attention_shift, heads_weight,
    query_bias, value_bias, merge_weight, merge_bias, feed_gain, feed_shift, up_weight, up_bias,
    down_weight, down_bias, bias_table,
):
    owners = lax.axis_size("dp")
    me = lax.axis_index("dp")
    part = C // owners
    is_second = lax.axis_index("section") == 1
    micro = images.shape[0]
    live_rows = (jnp.arange(images.shape[1], dtype=jnp.int32)[None, :] < counts).astype(F32)

    tiles = jnp.concatenate(
        [
            heads_weight[0].reshape(part, 3, C).transpose(1, 0, 2),
            merge_weight[0][None],
            up_weight[0].reshape(part, 4, C).transpose(1, 0, 2),
            down_weight[0].reshape(4, part, C),
        ]
    )
    vector = jnp.concatenate(
        [
            attention_gain[0], attention_shift[0], query_bias[0], value_bias[0], merge_bias[0],
            feed_gain[0], feed_shift[0], down_bias[0], up_bias[0],
        ]
    )
    vectors = lax.all_gather(vector, "dp", axis=0).astype(F32)
    weights = lax.all_gather(tiles, "dp", axis=0)
    wide = vectors[:, : 8 * part].reshape(owners, 8, part).transpose(1, 0, 2).reshape(8, C)
    up_row = vectors[:, 8 * part :].reshape(1, FF)
    vec = wide[jnp.array([0, 1, 4, 5, 6, 7, 7, 7])]
    project_row = jnp.concatenate([wide[2], jnp.zeros_like(wide[2]), wide[3]])[None]

    token = token_of_row(is_second)
    perm = (token[:, None] == jnp.arange(TOKIMG, dtype=jnp.int32)[None, :]).astype(BF16)
    permt = perm.T
    one_hot = (
        relative_index().reshape(-1)[:, None] == jnp.arange(TABLE, dtype=jnp.int32)[None, :]
    ).astype(F32)
    position = jnp.dot(one_hot, bias_table[0].astype(F32), precision=lax.Precision.HIGHEST)
    position = position.reshape(WT, WT, HEADS).transpose(2, 0, 1)
    position = pad_pairs(position).reshape(GROUPS, 4, PW, PW).transpose(0, 2, 1, 3)
    mask = pad_pairs(-100.0 * is_second.astype(F32) * shift_mask.astype(F32))
    edge = jnp.where(jnp.arange(PW) < WT, 0.0, -1e30)[:, None, None]
    bias = position[None] + mask[:, None, :, None, :] + edge
    bias = bias.reshape(NWIN * GROUPS, PW, 4 * PW)

    tick_bf16 = jnp.zeros((TOKIMG, C), BF16)
    received = tick_bf16
    kept, outputs = [], []
    layer_flops = 2 * ROWS * C * C * TILES
    for tick in range(micro + 1):
        own = images[tick, 0] if tick < micro else tick_bf16
        first = live_rows[tick, 0] if tick < micro else 0.0
        second = live_rows[tick - 1, 0] if tick > 0 else 0.0
        live = jnp.where(is_second, second, first).reshape(1, 1)
        source = jnp.where(is_second, received, own)
        out, *stored = call(
            forward_body,
            [
                ((TOKIMG, C), BF16), ((ROWS, C), BF16), ((ROWS, C), BF16), ((ROWS, 3 * C), BF16),
                ((NWIN * GROUPS, PW, 4 * PW), BF16), ((ROWS, C), BF16), ((ROWS, C), F32),
                ((ROWS, C), BF16), ((ROWS, FF), BF16), ((ROWS, FF), BF16),
            ],
            (source, live, perm, permt, bias, weights, vec, project_row, up_row),
            smem=(1,),
            flops=layer_flops,
        )
        kept.append((stored, live))
        outputs.append(out)
        if tick < micro:
            received = lax.ppermute(out, "section", [(0, 1)])
    layer_outputs = jnp.stack(
        [jnp.where(is_second, outputs[m + 1], outputs[m]) for m in range(micro)]
    )[None, :, None]

    received = tick_bf16
    products, grads = [], []
    vec_total = up_total = pair_total = 0.0
    for turn in range(micro + 1):
        (xw, h, qkv, a, r, x1, h2, z, gp), live = kept[micro - turn]
        own = cotangent[micro - 1 - turn, 0] if turn < micro else tick_bf16
        upstream = jnp.where(is_second, own, received)
        dx, sent, do, dg, db, dp, vg, ug, ds = call(
            backward_body,
            [
                ((TOKIMG, C), F32), ((TOKIMG, C), BF16), ((ROWS, C), BF16), ((ROWS, FF), BF16),
                ((ROWS, C), BF16), ((ROWS, 3 * C), BF16), ((8, C), F32), ((1, FF), F32),
                ((GROUPS, PW, 4 * PW), F32),
            ],
            (upstream, live, perm, permt, weights, vec, xw, qkv, a, x1, gp),
            scratch=(pltpu.VMEM((ROWS, C), BF16),),
            smem=(1,),
            flops=layer_flops,
        )
        products.append((h, r, h2, z, do, dg, db, dp))
        vec_total, up_total, pair_total = vec_total + vg, up_total + ug, pair_total + ds
        grads.append(jnp.where(is_second, sent.astype(F32), dx))
        if turn < micro:
            received = lax.ppermute(sent, "section", [(1, 0)])
    input_grads = jnp.stack(
        [
            jnp.where(is_second, grads[micro - 1 - m], grads[micro - m]) for m in range(micro)
        ]
    )[None, :, None]

    count = micro + 1
    (tile_grads,) = call(
        lambda *refs: weight_grads_body(count, *refs),
        [((owners, TILES, part, C), BF16)],
        tuple(p[i] for i in range(8) for p in products),
        flops=layer_flops * count,
    )
    own_tiles = lax.psum_scatter(tile_grads, "dp", scatter_dimension=0, tiled=False).astype(F32)

    pairs = pair_total.reshape(GROUPS, PW, 4, PW)[:, :WT, :, :WT]
    pairs = pairs.transpose(3, 1, 0, 2).reshape(WT * WT, HEADS)
    table = jnp.dot(one_hot.T, pairs, precision=lax.Precision.HIGHEST)
    flat = jnp.concatenate([vec_total.reshape(-1), up_total.reshape(-1), table.reshape(-1)])
    flat = lax.psum(flat, "dp")
    own_vec = lax.dynamic_slice(flat[: 8 * C].reshape(8, C), (0, me * part), (8, part))
    own_up = lax.dynamic_slice(flat[8 * C : 8 * C + FF], (me * (FF // owners),), (FF // owners,))
    table = flat[8 * C + FF :].reshape(1, TABLE, HEADS)
    return (
        layer_outputs,
        input_grads,
        own_vec[0][None],
        own_vec[1][None],
        own_tiles[0:3].transpose(1, 0, 2).reshape(1, part, 3 * C),
        own_vec[2][None],
        own_vec[3][None],
        own_tiles[3][None],
        own_vec[4][None],
        own_vec[5][None],
        own_vec[6][None],
        own_tiles[4:8].transpose(1, 0, 2).reshape(1, part, FF),
        own_up[None],
        own_tiles[8:12].reshape(1, 4 * part, C),
        own_vec[7][None],
        table,
    )


def solution(mesh):
    rows, matrix = P("section", "dp"), P("section", "dp", None)
    tokens = P("section", None, "dp", None, None)
    table = P("section", None, None)
    images = P(None, "dp", None, None)
    return jax.shard_map(
        shards,
        mesh=mesh,
        in_specs=(
            images, P(None, "dp"), P(), images, rows, rows, matrix, rows, rows, matrix, rows,
            rows, rows, matrix, rows, matrix, rows, table,
        ),
        out_specs=(
            tokens, tokens, rows, rows, matrix, rows, rows, matrix, rows, rows, rows, matrix,
            rows, matrix, rows, table,
        ),
        check_vma=False,
    )
```

time: 1080 us -> 428 us (0.40)
  local copies, waits for them, and re-layouts: 304 us -> 26.1 us
  matrix products: 188 us -> 2.91 us
  waiting for transfers between devices: 263 us -> 105 us
  Pallas kernels: 0 us -> 119 us
  blocking collectives: 196 us -> 119 us
  other arithmetic: 79.7 us -> 13.1 us
    reduce_scatter x4 -> x1, waiting for transfers between devices: 240 us -> 57.6 us  [shards(): lax.psum_scatter(tile_grads, 'dp', scatter_dimension=0, tiled=False)]
    dot_general x91 -> x2, matrix products: 169 us -> 2.91 us  [the longest x1 2.13 us: shards(): table = jnp.dot(one_hot.T, pairs, precision=lax.Precision.HIGHEST)]
    unnamed x2 -> x0, blocking collectives: 119 us -> none
    pallas_call x0 -> x11, Pallas kernels: none -> 119 us  [call(): pl.pallas_call(body, out_shape=[jax.ShapeDtypeStruct(s, d) for s, d in ou...]
    reshape x44 -> x10, local copies, waits for them, and re-layouts: 83.1 us -> 2.42 us  [the longest x1 0.88 us: shards(): own_tiles[4:8].transpose(1, 0, 2).reshape(1, part, FF)]
    psum x0 -> x1, blocking collectives: none -> 75.5 us  [shards(): flat = lax.psum(flat, 'dp')]
    another operation x31 -> x3, local copies, waits for them, and re-layouts: 74.9 us -> 2.99 us  [the longest x1 1.02 us: shards(): up_weight[0].reshape(part, 4, C).transpose(1, 0, 2)]
    unnamed x684 -> x96, local copies, waits for them, and re-layouts: 63.8 us -> 7.05 us
  transfers between devices with their start and end apart: 15 -> 10, of which waited for: 4 -> 7; matrix products, arithmetic and copies ran while one was open for 15% -> 6% of each run, Pallas kernels for 0% -> 0%
where the time goes in v1:
time: 428 us; the launch traced here: 419 us
  blocking collectives  119 us (28%)
  Pallas kernels  119 us (28%)
  waiting for transfers between devices  105 us (25%)
  local copies, waits for them, and re-layouts  26.1 us (6%)
  between operations  20.7 us (5%)
  starting transfers between devices  14 us (3%)
  other arithmetic  13.1 us (3%)
    pallas_call x11, Pallas kernels, call(): pl.pallas_call(body, out_shape=[jax.ShapeDtypeStruct(s, d) for s, d in ou...  119 us
    psum x1, blocking collectives, shards(): flat = lax.psum(flat, 'dp')  75.5 us
    reduce_scatter x1, waiting for transfers between devices, shards(): lax.psum_scatter(tile_grads, 'dp', scatter_dimension=0, tiled=False)  57.6 us
    all_gather x1, blocking collectives, shards(): vectors = lax.all_gather(vector, 'dp', axis=0).astype(F32)  43.1 us
    all_gather x1, waiting for transfers between devices, shards(): weights = lax.all_gather(tiles, 'dp', axis=0)  38.4 us
    ppermute x4, waiting for transfers between devices, shards(): received = lax.ppermute(sent, 'section', [(1, 0)])  8.65 us
  transfers between devices with their start and end apart: 10, of which 7 were waited for; matrix products, arithmetic and copies ran while one was open for 6% of the time, Pallas kernels for 0%

profile of v1, /device:TPU:0, one launch (start us, length us, event | category | flops | bytes accessed | tf_op | source)
XLA Modules:
  0.0 419.4 jit_solution(1190654791679616116)
XLA Ops:
  12.8 43.1 %all-gather.2 = bf16[16,1,384]{2,1,0:T(2,128)(2,1)S(1)} all-gather(bf16[1,1,384]{2,1,0:T(2,128)(2,1)S(1)} %reshape.327), channel_id=3, replica_groups=mesh['section'=2,'dp'=16] {'dp'}, dimensions={0}, use_global_device_ids=true | all-gather | bytes 13056 | tf_op jit(solution)/shard_map/all_gather | solution.py:286
  64.4 3.7 fusion.28
  71.2 38.4 %all-gather.5.cloned.1.call-done = bf16[192,32,512]{2,1,0:T(8,128)(2,1)} async-done(((bf16[12,32,512]{2,1,0:T(8,128)(2,1)}), bf16[192,32,512]{2,1,0:T(8,128)(2,1)}) %all-gather.5.cloned.1.call-update) | async-done | bytes 6291472 | tf_op jit(solution)/shard_map/all_gather | solution.py:287
  109.7 8.7 %shard_map.306 = (bf16[196,512]{1,0:T(8,128)(2,1)}, bf16[256,512]{1,0:T(8,128)(2,1)}, bf16[256,512]{1,0:T(8,128)(2,1)}, bf16[256,1536]{1,0:T(8,128)(2,1)}, bf16[...) custom-call(bf16[196,512]{1,0:T(8,128)(2,1)} %get-tuple-element.317., ...), custom_call_target="tpu_custom_call" | custom-call | flops 1610612736 | bytes 16777216 | tf_op jit(solution)/shard_map/pallas_call | solution.py:221
  121.9 8.8 %shard_map.307 = (bf16[196,512]{1,0:T(8,128)(2,1)}, bf16[256,512]{1,0:T(8,128)(2,1)}, bf16[256,512]{1,0:T(8,128)(2,1)}, bf16[256,1536]{1,0:T(8,128)(2,1)}, bf16[...) custom-call(bf16[196,512]{1,0:T(8,128)(2,1)} %fusion.18.x_ref, ...), custom_call_target="tpu_custom_call" | custom-call | flops 1610612736 | bytes 16777216 | tf_op jit(solution)/shard_map/pallas_call | solution.py:221
  134.8 8.7 %shard_map.308 = (bf16[196,512]{1,0:T(8,128)(2,1)}, bf16[256,512]{1,0:T(8,128)(2,1)}, bf16[256,512]{1,0:T(8,128)(2,1)}, bf16[256,1536]{1,0:T(8,128)(2,1)}, bf16[...) custom-call(bf16[196,512]{1,0:T(8,128)(2,1)} %fusion.17.x_ref, ...), custom_call_target="tpu_custom_call" | custom-call | flops 1610612736 | bytes 16777216 | tf_op jit(solution)/shard_map/pallas_call | solution.py:221
  143.5 2.2 collective-permute-start.2
  147.8 8.9 %shard_map.309 = (bf16[196,512]{1,0:T(8,128)(2,1)}, bf16[256,512]{1,0:T(8,128)(2,1)}, bf16[256,512]{1,0:T(8,128)(2,1)}, bf16[256,1536]{1,0:T(8,128)(2,1)}, bf16[...) custom-call(bf16[196,512]{1,0:T(8,128)(2,1)} %fusion.16.x_ref, ...), custom_call_target="tpu_custom_call" | custom-call | flops 1610612736 | bytes 16777216 | tf_op jit(solution)/shard_map/pallas_call | solution.py:221
  156.6 2.6 collective-permute-start.3
  160.8 8.7 %shard_map.310 = (bf16[196,512]{1,0:T(8,128)(2,1)}, bf16[256,512]{1,0:T(8,128)(2,1)}, bf16[256,512]{1,0:T(8,128)(2,1)}, bf16[256,1536]{1,0:T(8,128)(2,1)}, bf16[...) custom-call(bf16[196,512]{1,0:T(8,128)(2,1)} %broadcast_select_fusio, ...), custom_call_target="tpu_custom_call" | custom-call | flops 1610612736 | bytes 16777216 | tf_op jit(solution)/shard_map/pallas_call | solution.py:221
  169.5 11.5 %shard_map.311 = (f32[196,512]{1,0:T(8,128)}, bf16[196,512]{1,0:T(8,128)(2,1)}, bf16[256,512]{1,0:T(8,128)(2,1)}, bf16[256,2048]{1,0:T(8,128)(2,1)}, bf16[256,51...) custom-call(bf16[196,512]{1,0:T(8,128)(2,1)} %get-tuple-element.316., ...), custom_call_target="tpu_custom_call" | custom-call | flops 1610612736 | bytes 16777216 | tf_op jit(solution)/shard_map/pallas_call | solution.py:221
  182.5 2.1 collective-permute-done.4
  185.3 11.5 %shard_map.312 = (f32[196,512]{1,0:T(8,128)}, bf16[196,512]{1,0:T(8,128)(2,1)}, bf16[256,512]{1,0:T(8,128)(2,1)}, bf16[256,2048]{1,0:T(8,128)(2,1)}, bf16[256,51...) custom-call(bf16[196,512]{1,0:T(8,128)(2,1)} %fusion.13.e_ref, ...), custom_call_target="tpu_custom_call" | custom-call | flops 1610612736 | bytes 16777216 | tf_op jit(solution)/shard_map/pallas_call | solution.py:221
  198.1 2.3 collective-permute-done.5
  201.1 11.4 %shard_map.313 = (f32[196,512]{1,0:T(8,128)}, bf16[196,512]{1,0:T(8,128)(2,1)}, bf16[256,512]{1,0:T(8,128)(2,1)}, bf16[256,2048]{1,0:T(8,128)(2,1)}, bf16[256,51...) custom-call(bf16[196,512]{1,0:T(8,128)(2,1)} %fusion.14.e_ref, ...), custom_call_target="tpu_custom_call" | custom-call | flops 1610612736 | bytes 16777216 | tf_op jit(solution)/shard_map/pallas_call | solution.py:221
  213.8 2.3 collective-permute-done.6
  216.8 11.4 %shard_map.314 = (f32[196,512]{1,0:T(8,128)}, bf16[196,512]{1,0:T(8,128)(2,1)}, bf16[256,512]{1,0:T(8,128)(2,1)}, bf16[256,2048]{1,0:T(8,128)(2,1)}, bf16[256,51...) custom-call(bf16[196,512]{1,0:T(8,128)(2,1)} %fusion.15.e_ref, ...), custom_call_target="tpu_custom_call" | custom-call | flops 1610612736 | bytes 16777216 | tf_op jit(solution)/shard_map/pallas_call | solution.py:221
  229.8 2.0 collective-permute-done.7
  232.5 11.5 %shard_map.315 = (f32[196,512]{1,0:T(8,128)}, bf16[196,512]{1,0:T(8,128)(2,1)}, bf16[256,512]{1,0:T(8,128)(2,1)}, bf16[256,2048]{1,0:T(8,128)(2,1)}, bf16[256,51...) custom-call(bf16[196,512]{1,0:T(8,128)(2,1)} %broadcast_select_fusio, ...), custom_call_target="tpu_custom_call" | custom-call | flops 1610612736 | bytes 16777216 | tf_op jit(solution)/shard_map/pallas_call | solution.py:221
  244.0 18.0 %shard_map.316 = bf16[16,12,32,512]{3,2,1,0:T(8,128)(2,1)} custom-call(bf16[256,512]{1,0:T(8,128)(2,1)} %get-tuple-element.166.refs_0_, bf16[256,512]{1,0:T(8,128)(2,1)} %get-tuple-element.167.refs_1_, bf16[256,512]{1,0:T(8,128)(2,1)} %get-tuple-element.168.refs_2_, bf16[256,512]{1,0:T(8,128)(2,1)} %get-tuple-element.169.refs_3_, ...), custom_call_target="tpu_custom_call" | custom-call | flops 8053063680 | bytes 16777216 | tf_op jit(solution)/shard_map/pallas_call | solution.py:221
  265.6 2.1 fusion.5
  267.9 75.5 %psum.7 = f32[8848]{0:T(1024)S(1)} all-reduce(f32[8848]{0:T(1024)S(1)} %pad_maximum_fusion.1), channel_id=1, replica_groups=mesh['section'=2,'dp'=16] {'dp'}, use_global_device_ids=true, to_apply=%region_0.1 | all-reduce | flops 8848 | bytes 70784 | tf_op jit(solution)/shard_map/psum | solution.py:379
  345.2 2.8 copy.128
  349.9 57.6 %reduce-scatter.2.cloned.1.call-done = bf16[1,12,32,512]{3,2,1,0:T(8,128)(2,1)} async-done(((bf16[16,12,32,512]{3,2,1,0:T(8,128)(2,1)}), bf16[1,12,32,512]{3,2,1,0:T(8,128)(2,1)}) %reduce-scatter.2.cloned.1.call-update) | async-done | bytes 393232 | tf_op jit(solution)/shard_map/reduce_scatter | solution.py:373
  (187 shorter events, 42.9 us)
Async XLA Ops:
  7.2 51.8 %copy-start = (bf16[1,169,16]{1,2,0:T(8,128)(2,1)S(1)}, bf16[1,169,16]{1,2,0:T(8,128)(2,1)}, u32[]{:S(2)}) copy-start(bf16[1,169,16]{1,2,0:T(8,128)(2,1)} %param.36) | copy-start | bytes 16228
  7.2 5.4 %copy-start.41 = (bf16[1,32]{1,0:T(2,128)(2,1)S(1)}, bf16[1,32]{1,0:T(2,128)(2,1)}, u32[]{:S(2)}) copy-start(bf16[1,32]{1,0:T(2,128)(2,1)} %param.35) | copy-start | bytes 196
  7.2 5.4 %copy-start.42 = (bf16[1,128]{1,0:T(2,128)(2,1)S(1)}, bf16[1,128]{1,0:T(2,128)(2,1)}, u32[]{:S(2)}) copy-start(bf16[1,128]{1,0:T(2,128)(2,1)} %param.33) | copy-start | bytes 772
  7.2 5.4 %copy-start.40 = (bf16[1,32]{1,0:T(2,128)(2,1)S(1)}, bf16[1,32]{1,0:T(2,128)(2,1)}, u32[]{:S(2)}) copy-start(bf16[1,32]{1,0:T(2,128)(2,1)} %param.31) | copy-start | bytes 196
  7.2 5.4 %copy-start.39 = (bf16[1,32]{1,0:T(2,128)(2,1)S(1)}, bf16[1,32]{1,0:T(2,128)(2,1)}, u32[]{:S(2)}) copy-start(bf16[1,32]{1,0:T(2,128)(2,1)} %param.30) | copy-start | bytes 196
  7.3 49.2 %copy-start.43 = (s32[4,1]{0,1:T(1,128)S(1)}, s32[4,1]{0,1:T(1,128)}, u32[]{:S(2)}) copy-start(s32[4,1]{0,1:T(1,128)} %param.20) | copy-start | bytes 52
  7.3 102.4 %all-gather.5.cloned.1.call-start = ((), (), s32[]{:S(2)}) async-start(), calls=%async_computation.2 | async-start | bytes 6684672 | tf_op jit(solution)/shard_map/all_gather | solution.py:287
  9.1 49.6 %copy-start.22 = (s32[4,49,49]{2,0,1:T(4,128)S(1)}, s32[4,49,49]{2,0,1:T(4,128)}, u32[]{:S(2)}) copy-start(s32[4,49,49]{2,0,1:T(4,128)} %param.21) | copy-start | bytes 115252
  12.6 395.0 %reduce-scatter.2.cloned.1.call-start = ((), (), s32[]{:S(2)}) async-start(), calls=%async_computation.1 | async-start | bytes 6684672 | tf_op jit(solution)/shard_map/reduce_scatter | solution.py:373
  118.4 2.8 collective-permute-start
  130.7 3.3 collective-permute-start.1
  143.5 3.5 collective-permute-start.2
  156.6 3.5 collective-permute-start.3
  181.0 3.6 collective-permute-start.4
  196.8 3.6 collective-permute-start.5
  212.5 3.6 collective-permute-start.6
  228.2 3.6 collective-permute-start.7
  265.3 78.1 %copy-start.4 = (f32[196,512]{1,0:T(8,128)S(1)}, f32[196,512]{1,0:T(8,128)}, u32[]{:S(2)}) copy-start(f32[196,512]{1,0:T(8,128)} %get-tuple-element.150) | copy-start | bytes 1204228
  265.3 78.1 %copy-start.5 = (f32[196,512]{1,0:T(8,128)S(1)}, f32[196,512]{1,0:T(8,128)}, u32[]{:S(2)}) copy-start(f32[196,512]{1,0:T(8,128)} %get-tuple-element.149) | copy-start | bytes 1204228
  265.3 78.1 %copy-start.6 = (f32[196,512]{1,0:T(8,128)S(1)}, f32[196,512]{1,0:T(8,128)}, u32[]{:S(2)}) copy-start(f32[196,512]{1,0:T(8,128)} %get-tuple-element.148) | copy-start | bytes 1204228
  265.3 78.1 %copy-start.7 = (f32[196,512]{1,0:T(8,128)S(1)}, f32[196,512]{1,0:T(8,128)}, u32[]{:S(2)}) copy-start(f32[196,512]{1,0:T(8,128)} %get-tuple-element.140) | copy-start | bytes 1204228
  265.4 78.1 %copy-start.8 = (f32[196,512]{1,0:T(8,128)S(1)}, f32[196,512]{1,0:T(8,128)}, u32[]{:S(2)}) copy-start(f32[196,512]{1,0:T(8,128)} %get-tuple-element.147) | copy-start | bytes 1204228
  265.4 78.1 %copy-start.19 = (bf16[196,512]{1,0:T(8,128)(2,1)S(1)}, bf16[196,512]{1,0:T(8,128)(2,1)}, u32[]{:S(2)}) copy-start(bf16[196,512]{1,0:T(8,128)(2,1)} %get-tuple-element.121) | copy-start | bytes 602116
  265.4 78.1 %copy-start.20 = (bf16[196,512]{1,0:T(8,128)(2,1)S(1)}, bf16[196,512]{1,0:T(8,128)(2,1)}, u32[]{:S(2)}) copy-start(bf16[196,512]{1,0:T(8,128)(2,1)} %get-tuple-element.127) | copy-start | bytes 602116
  (33 other events, 83.5 us)
Sparse Core Ops, SparseCore 0:
  12.7 96.9 all-gather.4
  262.2 145.3 reduce-scatter.1
